TPU v7x, 256 devices: a whole 4x4x8 slice. The times are simulated.
256 devices in a mesh: dp: 4 (over x), expert: 64 (over y, z, core).
Axes of the slice: x: 4, y: 4, z: 8, core: 2. Of those that a mesh axis runs over, the one named last changes fastest.
Arguments:
- tokens: bfloat16 [8192, 7168], P('expert', 'dp'), may hold values from -6 to 6
- gate_up: bfloat16 [64, 7168, 2, 1024], P('expert', 'dp'), may hold values from -0.0625 to 0.0625
- down: bfloat16 [64, 1024, 7168], P('expert', None, 'dp'), may hold values from -0.1875 to 0.1875
- route_ids: int32 [8192, 8], P('expert'), may hold values from 0 to 63, all different within a row; in each aligned block of 128 rows (0 to 127, 128 to 255, ...) at most 18 rows name the same one
- route_weight: bfloat16 [8192, 8], P('expert'), may hold values from 0.099609375 to 0.59765625
- swap_flags: int32 [64], replicated, may hold values from 0 to 1, as said below
Outputs:
- mixed: bfloat16 [8192, 7168], P('expert', 'dp')
Inputs may be any that keep to these rules, and one draw needn't show every extreme that they name: `route_ids`: each row names 8 different slots; among the 128 rows of one device no slot is named by more than 18 rows, a bound that some block reaches. swap_flags[j] equals swap_flags[j + 32] for every j below 32.
All inputs are finite; a program needn't handle non-finite values.
Results may differ from a plain program's by a relative error of at most 0.024.
Values may be sent and summed in bfloat16 or wider, within the bound.
No kernel may reach another device: no remote copies, remote signals or barrier semaphores. Data moves between devices by JAX's collectives and lax.ppermute only.
A program may use at most 128 MiB of HBM per device.

v0:
```python
import jax
import jax.numpy as jnp
from jax import lax
from jax.sharding import PartitionSpec as P

TOP = 8


def from_behind(block, axis, distance):
    devices = range(lax.axis_size(axis))
    route = [((i - distance) % len(devices), i) for i in devices]
    return lax.ppermute(block, axis, route)


def body(tokens, gate_up, down, route_ids, route_weight, swap_flags):
    members = lax.axis_size("expert")
    half_axis = members // 2
    tok_rows, feat_width = tokens.shape
    hidden_units = down.shape[1]
    capacity = min(tok_rows, 9 * tok_rows * TOP // (8 * members))
    own_gu = gate_up[0]
    own_dn = down[0]
    my_index = lax.axis_index("expert")
    slot_ids = jnp.arange(members, dtype=jnp.int32)
    flag_mine = jnp.sum(jnp.where(slot_ids == my_index, swap_flags, 0))
    far_gu, far_dn = from_behind((own_gu, own_dn), "expert", half_axis)
    use_gu = jnp.where(flag_mine == 1, far_gu, own_gu)
    use_dn = jnp.where(flag_mine == 1, far_dn, own_dn)
    flat_ids = route_ids.reshape(-1)
    onehot = (flat_ids[:, None] == slot_ids[None, :]).astype(jnp.int32)
    slot_rank = jnp.sum(jnp.cumsum(onehot, axis=0) * onehot, axis=1) - 1
    position = flat_ids * capacity + slot_rank
    pair_row = jnp.arange(flat_ids.shape[0], dtype=jnp.int32) // TOP
    source_row = jnp.full((members * capacity,), tok_rows, jnp.int32).at[position].set(pair_row)
    padded = jnp.concatenate([tokens, jnp.zeros((1, feat_width), tokens.dtype)], axis=0)
    outgoing = padded[source_row].reshape(members, capacity, feat_width)
    flat_gu = use_gu.reshape(feat_width, 2 * hidden_units)
    received = lax.all_to_all(outgoing, "expert", split_axis=0, concat_axis=0, tiled=True)
    senders, item_count, _ = received.shape
    row_block = received.reshape(senders * item_count, feat_width)
    partial_value = jnp.dot(row_block, flat_gu, preferred_element_type=jnp.float32).reshape(
        -1, 2, hidden_units
    )
    summed = lax.psum(partial_value.astype(jnp.bfloat16), "dp").astype(jnp.float32)
    hidden = (jax.nn.silu(summed[:, 0]) * summed[:, 1]).astype(jnp.bfloat16)
    result = jnp.dot(hidden, use_dn, preferred_element_type=jnp.float32).astype(jnp.bfloat16)
    result = result.reshape(senders, item_count, feat_width)
    returned_rows = lax.all_to_all(result, "expert", split_axis=0, concat_axis=0, tiled=True)
    picked = returned_rows.reshape(members * capacity, feat_width)[position]
    picked = picked.reshape(tok_rows, TOP, feat_width).astype(jnp.float32)
    mixed = jnp.sum(picked * route_weight.astype(jnp.float32)[..., None], axis=1)
    return mixed.astype(jnp.bfloat16)


def solution(mesh):
    return jax.shard_map(
        body,
        mesh=mesh,
        in_specs=(
            P("expert", "dp"),
            P("expert", "dp", None, None),
            P("expert", None, "dp"),
            P("expert", None),
            P("expert", None),
            P(),
        ),
        out_specs=P("expert", "dp"),
        check_vma=False,
    )
```

profile of v0, /device:TPU:1, one launch (start us, length us, event | category | flops | bytes accessed | tf_op | source)
XLA Modules:
  0.0 565.3 jit_solution(11097575957303755263)
XLA Ops:
  6.5 3.7 collective-permute-start
  10.3 0.8 copy.10
  11.1 0.1 eq.39
  11.2 0.1 eq.35
  11.2 0.7 broadcast_multiply_fusion
  12.0 18.0 %reduce-window.6 = s32[64,8,128]{2,1,0:T(8,128)S(1)} reduce-window(s32[64,8,128]{2,1,0:T(8,128)S(1)} %fusion.9, s32[]{:T(128)} %constant.37.clone.1), window={size=1x1x128 pad=0_0x0_0x127_0}, to_apply=%region_0.1 | reduce-window | flops 8323072 | bytes 524292 | tf_op jit(solution)/shard_map/reduce-window
  30.0 0.1 slice.20
  30.1 0.1 copy.12
  30.3 0.1 copy.13
  30.4 0.1 copy.9
  30.5 0.1 mul.36
  30.6 1.1 concatenate.3
  31.6 0.1 broadcast_add_fusion
  31.8 0.1 fusion.8
  31.9 4.3 scatter_custom_fusion
  36.2 5.7 %gather_fusion = bf16[1152,1792]{1,0:T(8,128)(2,1)} fusion(bf16[129,1792]{1,0:T(8,128)(2,1)S(1)} %concatenate.3, s32[2048]{0:T(1024)S(1)} %pad_clamp_fusion), kind=kCustom, calls=%fused_computation | custom fusion | bytes 8262144 | tf_op jit(solution)/shard_map/gather | solution.py:36
  41.9 7.2 %reshape.73 = bf16[64,18,1792]{2,1,0:T(8,128)(2,1)} reshape(bf16[1152,1792]{1,0:T(8,128)(2,1)} %gather_fusion) | data formatting | bytes 8257536 | tf_op jit(solution)/shard_map/reshape | solution.py:36
  49.1 0.0 copy-start.2
  49.1 10.8 %all-to-all-start = ((bf16[64,18,1792]{2,1,0:T(8,128)(2,1)}), bf16[64,18,1792]{2,1,0:T(8,128)(2,1)}, u32[]{:S(2)}, u32[]{:S(2)}) async-start(bf16[64,18,1792]{2,1,0:T(8,128)(2,1)} %reshape.73), calls=%async_computation | async-start | bytes 11010048 | tf_op jit(solution)/shard_map/all_to_all | solution.py:38
  59.9 0.0 all-reduce.3.cloned.1.call-start
  59.9 0.0 copy-done.2
  60.0 0.6 fusion.15
  61.2 159.2 %collective-permute-done = bf16[1792,2,1024]{2,1,0:T(2,128)(2,1)} collective-permute-done((bf16[1792,2,1024]{2,1,0:T(2,128)(2,1)}, bf16[1792,2,1024]{2,1,0:T(2,128)(2,1)}, u32[]{:S(2)}, u32[]{:S(2)}) %collective-permute-start) | collective-permute-done | bytes 7340064 | tf_op jit(solution)/shard_map/ppermute | solution.py:12
  220.4 9.2 %broadcast_select_fusion = bf16[1792,2,1024]{2,1,0:T(2,128)(2,1)S(1)} fusion(bf16[1792,2,1024]{2,1,0:T(2,128)(2,1)} %collective-permute-done, pred[]{:T(512)S(6)} %eq.45, bf16[1,1792,2,1024]{3,2,1,0:T(2,128)(2,1)} %param.7), kind=kLoop, calls=%fused_computation.3 | loop fusion | flops 3670016 | bytes 22020096 | tf_op jit(solution)/shard_map/jit(_where)/select_n | solution.py:27
  229.7 6.1 %copy.17 = bf16[224,8,2,1024]{3,1,2,0:T(8,128)(2,1)} copy(bf16[224,8,2,1024]{3,2,1,0:T(2,128)(2,1)S(1)} %bitcast.46) | data formatting | bytes 14680064
  235.8 10.0 %copy.14 = bf16[2048,1792]{1,0:T(8,128)(2,1)} copy(bf16[2048,1792]{0,1:T(8,128)(2,1)} %bitcast.45) | data formatting | bytes 14680064 | tf_op jit(solution)/shard_map/dot_general | solution.py:41
  245.8 0.0 all-to-all-done
  245.8 7.3 %reshape.104 = bf16[1152,1792,1]{1,0,2:T(8,128)(2,1)} reshape(bf16[64,18,1792]{2,1,0:T(8,128)(2,1)} %all-to-all-done) | data formatting | bytes 8257536 | tf_op jit(solution)/shard_map/reshape | solution.py:40
  253.2 13.7 %convolution_convert_fusion.1 = bf16[1152,2,1024]{2,0,1:T(8,128)(2,1)} fusion(bf16[1152,1792,1]{1,0,2:T(8,128)(2,1)} %reshape.104, bf16[2,1024,1792]{2,1,0:T(8,128)(2,1)} %bitcast.47), kind=kOutput, calls=%fused_computation.7 | convolution fusion | flops 8458076160 | bytes 16187392 | tf_op jit(solution)/shard_map/dot_general | solution.py:41
  266.9 0.0 all-reduce.3.cloned.1.call-update
  266.9 4.0 collective-permute-start.1
  270.9 108.6 %all-reduce.3.cloned.1.call-done = bf16[1152,2,1024]{2,0,1:T(8,128)(2,1)} async-done(((bf16[1152,2,1024]{2,0,1:T(8,128)(2,1)}), bf16[1152,2,1024]{2,0,1:T(8,128)(2,1)}) %all-reduce.3.cloned.1.call-update) | async-done | bytes 4718608 | tf_op jit(solution)/shard_map/psum | solution.py:44
  379.5 0.0 copy-start.1
  379.5 3.7 convert_element_type.31
  383.1 0.0 collective-permute-done.1
  383.2 0.0 copy-done.1
  383.2 8.9 %convolution_convert_fusion = bf16[1152,1792]{1,0:T(8,128)(2,1)} fusion(bf16[1024,1792]{1,0:T(8,128)(2,1)} %collective-permute-done.1, pred[]{:T(512)S(6)} %eq.45, f32[1152,2,1024]{2,0,1:T(8,128)S(1)} %convert_element_type.31, bf16[1,1024,1792]{2,1,0:T(8,128)(2,1)S(1)} %copy-done.1), kind=kOutput, calls=%fused_computation.4 | convolution fusion | flops 4238835712 | bytes 20905984 | tf_op jit(solution)/shard_map/dot_general | solution.py:46
  392.1 7.3 %reshape.76 = bf16[64,18,1792]{2,1,0:T(8,128)(2,1)} reshape(bf16[1152,1792]{1,0:T(8,128)(2,1)} %convolution_convert_fusion) | data formatting | bytes 8257536 | tf_op jit(solution)/shard_map/reshape | solution.py:47
  399.3 0.0 copy-start
  399.3 11.0 %all-to-all-start.1 = ((bf16[64,18,1792]{2,1,0:T(8,128)(2,1)}), bf16[64,18,1792]{2,1,0:T(8,128)(2,1)}, u32[]{:S(2)}, u32[]{:S(2)}) async-start(bf16[64,18,1792]{2,1,0:T(8,128)(2,1)} %reshape.76), calls=%async_computation.1 | async-start | bytes 11010048 | tf_op jit(solution)/shard_map/all_to_all | solution.py:48
  410.3 0.0 copy-done
  410.3 0.1 copy.15
  410.5 123.9 %all-to-all-done.1 = bf16[64,18,1792]{2,1,0:T(8,128)(2,1)} async-done(((bf16[64,18,1792]{2,1,0:T(8,128)(2,1)}), bf16[64,18,1792]{2,1,0:T(8,128)(2,1)}, u32[]{:S(2)}, u32[]{:S(2)}) %all-to-all-start.1) | async-done | bytes 4128800 | tf_op jit(solution)/shard_map/all_to_all | solution.py:48
  534.3 7.3 %reshape.77 = bf16[1152,1792]{1,0:T(8,128)(2,1)} reshape(bf16[64,18,1792]{2,1,0:T(8,128)(2,1)} %all-to-all-done.1) | data formatting | bytes 8257536 | tf_op jit(solution)/shard_map/reshape | solution.py:49
  541.7 10.6 %gather_fusion.1 = bf16[1024,1792]{1,0:T(8,128)(2,1)} fusion(bf16[1152,1792]{1,0:T(8,128)(2,1)} %reshape.77, s32[1024]{0:T(1024)S(1)} %broadcast_clamp_fusion), kind=kCustom, calls=%fused_computation.1 | custom fusion | bytes 7344128 | tf_op jit(solution)/shard_map/gather | solution.py:49
  552.3 6.1 %fusion = bf16[128,1792]{1,0:T(8,128)(2,1)} fusion(bf16[1024,1792]{1,0:T(8,128)(2,1)} %gather_fusion.1, f32[128,8]{1,0:T(8,128)S(1)} %copy.15), kind=kLoop, calls=%fused_computation.6 | loop fusion | flops 5275648 | bytes 4132864 | tf_op jit(solution)/shard_map/reduce_sum | solution.py:51
  (9 shorter events, 0.1 us)
Async XLA Ops:
  6.5 213.9 %collective-permute-start = (bf16[1792,2,1024]{2,1,0:T(2,128)(2,1)}, bf16[1792,2,1024]{2,1,0:T(2,128)(2,1)}, u32[]{:S(2)}, u32[]{:S(2)}) collective-permute-start(bf16[1792,2,1024]{2,1,0:T(2,128)(2,1)} %bitcast.48), channel_id=1, source_target_pairs={{32,0},{33,1},{34,2},{35,3},{36,4},{37,5},{38,6},{39,7},{40,8},{41... | collective-permute-start | bytes 22020104 | tf_op jit(solution)/shard_map/ppermute | solution.py:12
  49.1 10.8 %copy-start.2 = (s32[64]{0:T(128)S(1)}, s32[64]{0:T(128)}, u32[]{:S(2)}) copy-start(s32[64]{0:T(128)} %param.11) | copy-start | bytes 772
  49.1 196.7 %all-to-all-start = ((bf16[64,18,1792]{2,1,0:T(8,128)(2,1)}), bf16[64,18,1792]{2,1,0:T(8,128)(2,1)}, u32[]{:S(2)}, u32[]{:S(2)}) async-start(bf16[64,18,1792]{2,1,0:T(8,128)(2,1)} %reshape.73), calls=%async_computation | async-start | bytes 11010048 | tf_op jit(solution)/shard_map/all_to_all | solution.py:38
  59.9 319.6 %all-reduce.3.cloned.1.call-start = ((), (), s32[]{:S(2)}) async-start(), calls=%async_computation.2 | async-start | bytes 9437184 | tf_op jit(solution)/shard_map/psum | solution.py:44
  266.9 116.2 %collective-permute-start.1 = (bf16[1024,1792]{1,0:T(8,128)(2,1)}, bf16[1024,1792]{1,0:T(8,128)(2,1)}, u32[]{:S(2)}, u32[]{:S(2)}) collective-permute-start(bf16[1024,1792]{1,0:T(8,128)(2,1)} %bitcast.54), channel_id=1, source_target_pairs={{32,0},{33,1},{34,2},{35,3},{36,4},{37,5},{38,6},{39,7},{40,8},{41... | collective-permute-start | bytes 11010056 | tf_op jit(solution)/shard_map/ppermute | solution.py:12
  379.5 3.7 copy-start.1
  399.3 11.0 %copy-start = (bf16[128,8]{0,1:T(8,128)(2,1)S(1)}, bf16[128,8]{0,1:T(8,128)(2,1)}, u32[]{:S(2)}) copy-start(bf16[128,8]{0,1:T(8,128)(2,1)} %param.10) | copy-start | bytes 6148
  399.3 135.0 %all-to-all-start.1 = ((bf16[64,18,1792]{2,1,0:T(8,128)(2,1)}), bf16[64,18,1792]{2,1,0:T(8,128)(2,1)}, u32[]{:S(2)}, u32[]{:S(2)}) async-start(bf16[64,18,1792]{2,1,0:T(8,128)(2,1)} %reshape.76), calls=%async_computation.1 | async-start | bytes 11010048 | tf_op jit(solution)/shard_map/all_to_all | solution.py:48
Sparse Core Ops, SparseCore 0:
  267.0 112.3 all-reduce.2
where the time goes:
time: 567 us; the launch traced here: 565 us
  waiting for transfers between devices  392 us (69%)
  local copies, waits for them, and re-layouts  68.6 us (12%)
  other arithmetic  38.6 us (7%)
  starting transfers between devices  29.5 us (5%)
  matrix products  22.6 us (4%)
  between operations  14.2 us (3%)
    ppermute x2, waiting for transfers between devices, from_behind(): return lax.ppermute(block, axis, route)  159 us
    all_to_all x1, waiting for transfers between devices, body(): lax.all_to_all(result, 'expert', split_axis=0, concat_axis=0, tiled=True)  124 us
    psum x1, waiting for transfers between devices, body(): lax.psum(partial_value.astype(jnp.bfloat16), 'dp').astype(jnp.float32)  109 us
    another operation x3, other arithmetic  18.2 us
    dot_general x1, matrix products, body(): jnp.dot(row_block, flat_gu, preferred_element_type=jnp.float32)  13.7 us
  transfers between devices with their start and end apart: 5, of which 3 were waited for; matrix products, arithmetic and copies ran while one was open for 12% of the time, Pallas kernels for 0%

commit v1 on v0

--- a/solution.py
+++ b/solution.py
@@ -6,27 +6,18 @@
 TOP = 8
 
 
-def from_behind(block, axis, distance):
-    devices = range(lax.axis_size(axis))
-    route = [((i - distance) % len(devices), i) for i in devices]
-    return lax.ppermute(block, axis, route)
-
-
 def body(tokens, gate_up, down, route_ids, route_weight, swap_flags):
     members = lax.axis_size("expert")
     half_axis = members // 2
     tok_rows, feat_width = tokens.shape
     hidden_units = down.shape[1]
     capacity = min(tok_rows, 9 * tok_rows * TOP // (8 * members))
-    own_gu = gate_up[0]
-    own_dn = down[0]
-    my_index = lax.axis_index("expert")
+    use_gu = gate_up[0]
+    use_dn = down[0]
     slot_ids = jnp.arange(members, dtype=jnp.int32)
-    flag_mine = jnp.sum(jnp.where(slot_ids == my_index, swap_flags, 0))
-    far_gu, far_dn = from_behind((own_gu, own_dn), "expert", half_axis)
-    use_gu = jnp.where(flag_mine == 1, far_gu, own_gu)
-    use_dn = jnp.where(flag_mine == 1, far_dn, own_dn)
-    flat_ids = route_ids.reshape(-1)
+    source_slot = jnp.where(swap_flags == 1, (slot_ids + half_axis) % members, slot_ids)
+    new_ids = route_ids.reshape(-1)
+    flat_ids = jnp.sum(jnp.where(new_ids[:, None] == slot_ids[None, :], source_slot[None, :], 0), axis=1)
     onehot = (flat_ids[:, None] == slot_ids[None, :]).astype(jnp.int32)
     slot_rank = jnp.sum(jnp.cumsum(onehot, axis=0) * onehot, axis=1) - 1
     position = flat_ids * capacity + slot_rank

time: 567 us -> 491 us (0.87)
  waiting for transfers between devices: 392 us -> 331 us
  other arithmetic: 38.6 us -> 28.9 us
    ppermute x2 -> x0, waiting for transfers between devices: 159 us -> none  [from_behind(): return lax.ppermute(block, axis, route)]
    all_to_all x1, waiting for transfers between devices: 0.01 us -> 105 us  [body(): lax.all_to_all(outgoing, 'expert', split_axis=0, concat_axis=0, tiled=True)]
    select_n x1, other arithmetic: 9.23 us -> 0.66 us  [body(): jnp.where(swap_flags == 1, (slot_ids + half_axis) % members, slot_ids)]
    ppermute x2 -> x0, starting transfers between devices: 7.73 us -> none  [from_behind(): return lax.ppermute(block, axis, route)]
  transfers between devices with their start and end apart: 5 -> 3, of which waited for: 3 -> 3; matrix products, arithmetic and copies ran while one was open for 12% -> 4% of each run, Pallas kernels for 0% -> 0%
where the time goes in v1:
time: 491 us; the launch traced here: 490 us
  waiting for transfers between devices  331 us (67%)
  local copies, waits for them, and re-layouts  71.4 us (15%)
  other arithmetic  28.9 us (6%)
  starting transfers between devices  24.5 us (5%)
  matrix products  20.3 us (4%)
  between operations  13.5 us (3%)
    all_to_all x1, waiting for transfers between devices, body(): lax.all_to_all(result, 'expert', split_axis=0, concat_axis=0, tiled=True)  124 us
    all_to_all x1, waiting for transfers between devices, body(): lax.all_to_all(outgoing, 'expert', split_axis=0, concat_axis=0, tiled=True)  105 us
    psum x1, waiting for transfers between devices, body(): lax.psum(partial_value.astype(jnp.bfloat16), 'dp').astype(jnp.float32)  103 us
    another operation x3, other arithmetic  18.2 us
    dot_general x1, matrix products, body(): jnp.dot(row_block, flat_gu, preferred_element_type=jnp.float32)  13.7 us
    all_to_all x1, starting transfers between devices, body(): lax.all_to_all(outgoing, 'expert', split_axis=0, concat_axis=0, tiled=True)  13.3 us
    all_to_all x1, starting transfers between devices, body(): lax.all_to_all(result, 'expert', split_axis=0, concat_axis=0, tiled=True)  11 us
    gather x1, local copies, waits for them, and re-layouts, body(): picked = returned_rows.reshape(members * capacity, feat_width)[position]  10.6 us
  transfers between devices with their start and end apart: 3, of which 3 were waited for; matrix products, arithmetic and copies ran while one was open for 4% of the time, Pallas kernels for 0%

profile of v1, /device:TPU:1, one launch (start us, length us, event | category | flops | bytes accessed | tf_op | source)
XLA Modules:
  0.0 490.1 jit_solution(5888665559641969009)
XLA Ops:
  6.5 0.8 copy.9
  7.3 0.1 eq.46
  7.4 0.7 compare_select_fusion.4
  8.1 0.1 select_reduce_fusion
  8.2 18.0 %reduce-window.6 = s32[64,8,128]{2,1,0:T(8,128)S(1)} reduce-window(s32[64,8,128]{2,1,0:T(8,128)S(1)} %fusion.7, s32[]{:T(128)} %constant.48.clone.1), window={size=1x1x128 pad=0_0x0_0x127_0}, to_apply=%region_1.2 | reduce-window | flops 8323072 | bytes 524292 | tf_op jit(solution)/shard_map/reduce-window
  26.2 0.1 slice.20
  26.4 0.1 copy.10
  26.5 0.1 copy.11
  26.6 0.1 broadcast_add_fusion
  26.8 0.1 fusion.6
  26.9 4.3 scatter_custom_fusion
  31.2 1.1 concatenate.3
  32.3 5.7 %gather_fusion = bf16[1152,1792]{1,0:T(8,128)(2,1)} fusion(bf16[129,1792]{1,0:T(8,128)(2,1)S(1)} %concatenate.3, s32[2048]{0:T(1024)S(1)} %pad_clamp_fusion), kind=kCustom, calls=%fused_computation | custom fusion | bytes 8262144 | tf_op jit(solution)/shard_map/gather | solution.py:27
  37.9 7.2 %reshape.69 = bf16[64,18,1792]{2,1,0:T(8,128)(2,1)} reshape(bf16[1152,1792]{1,0:T(8,128)(2,1)} %gather_fusion) | data formatting | bytes 8257536 | tf_op jit(solution)/shard_map/reshape | solution.py:27
  45.2 13.3 %all-to-all-start = ((bf16[64,18,1792]{2,1,0:T(8,128)(2,1)}), bf16[64,18,1792]{2,1,0:T(8,128)(2,1)}, u32[]{:S(2)}, u32[]{:S(2)}) async-start(bf16[64,18,1792]{2,1,0:T(8,128)(2,1)} %reshape.69), calls=%async_computation | async-start | bytes 11010048 | tf_op jit(solution)/shard_map/all_to_all | solution.py:29
  58.5 0.2 all-reduce.3.cloned.1.call-start
  58.7 9.2 %copy.15 = bf16[224,8,2,1024]{3,1,2,0:T(8,128)(2,1)} copy(bf16[224,8,2,1024]{3,2,1,0:T(2,128)(2,1)} %bitcast.35) | data formatting | bytes 14680064
  67.9 10.0 %copy.12 = bf16[2048,1792]{1,0:T(8,128)(2,1)} copy(bf16[2048,1792]{0,1:T(8,128)(2,1)} %bitcast.34) | data formatting | bytes 14680064 | tf_op jit(solution)/shard_map/dot_general | solution.py:32
  77.9 104.5 %all-to-all-done = bf16[64,18,1792]{2,1,0:T(8,128)(2,1)} async-done(((bf16[64,18,1792]{2,1,0:T(8,128)(2,1)}), bf16[64,18,1792]{2,1,0:T(8,128)(2,1)}, u32[]{:S(2)}, u32[]{:S(2)}) %all-to-all-start) | async-done | bytes 4128800 | tf_op jit(solution)/shard_map/all_to_all | solution.py:29
  182.5 7.3 %reshape.99 = bf16[1152,1792,1]{1,0,2:T(8,128)(2,1)} reshape(bf16[64,18,1792]{2,1,0:T(8,128)(2,1)} %all-to-all-done) | data formatting | bytes 8257536 | tf_op jit(solution)/shard_map/reshape | solution.py:31
  189.8 13.7 %convolution_convert_fusion.1 = bf16[1152,2,1024]{2,0,1:T(8,128)(2,1)} fusion(bf16[1152,1792,1]{1,0,2:T(8,128)(2,1)} %reshape.99, bf16[2,1024,1792]{2,1,0:T(8,128)(2,1)} %bitcast.36), kind=kOutput, calls=%fused_computation.6 | convolution fusion | flops 8458076160 | bytes 16187392 | tf_op jit(solution)/shard_map/dot_general | solution.py:32
  203.6 0.0 all-reduce.3.cloned.1.call-update
  203.6 103.1 %all-reduce.3.cloned.1.call-done = bf16[1152,2,1024]{2,0,1:T(8,128)(2,1)} async-done(((bf16[1152,2,1024]{2,0,1:T(8,128)(2,1)}), bf16[1152,2,1024]{2,0,1:T(8,128)(2,1)}) %all-reduce.3.cloned.1.call-update) | async-done | bytes 4718608 | tf_op jit(solution)/shard_map/psum | solution.py:35
  306.6 0.0 copy-start.1
  306.6 3.7 convert_element_type.34
  310.3 0.0 copy-done.1
  310.3 6.6 %convolution_convert_fusion = bf16[1152,1792]{1,0:T(8,128)(2,1)} fusion(bf16[1,1024,1792]{2,1,0:T(8,128)(2,1)S(1)} %copy-done.1, f32[1152,2,1024]{2,0,1:T(8,128)S(1)} %convert_element_type.34), kind=kOutput, calls=%fused_computation.3 | convolution fusion | flops 4237000704 | bytes 17235968 | tf_op jit(solution)/shard_map/dot_general | solution.py:37
  317.0 7.3 %reshape.71 = bf16[64,18,1792]{2,1,0:T(8,128)(2,1)} reshape(bf16[1152,1792]{1,0:T(8,128)(2,1)} %convolution_convert_fusion) | data formatting | bytes 8257536 | tf_op jit(solution)/shard_map/reshape | solution.py:38
  324.2 0.0 copy-start
  324.2 11.0 %all-to-all-start.1 = ((bf16[64,18,1792]{2,1,0:T(8,128)(2,1)}), bf16[64,18,1792]{2,1,0:T(8,128)(2,1)}, u32[]{:S(2)}, u32[]{:S(2)}) async-start(bf16[64,18,1792]{2,1,0:T(8,128)(2,1)} %reshape.71), calls=%async_computation.1 | async-start | bytes 11010048 | tf_op jit(solution)/shard_map/all_to_all | solution.py:39
  335.2 0.0 copy-done
  335.2 0.1 copy.13
  335.3 123.9 %all-to-all-done.1 = bf16[64,18,1792]{2,1,0:T(8,128)(2,1)} async-done(((bf16[64,18,1792]{2,1,0:T(8,128)(2,1)}), bf16[64,18,1792]{2,1,0:T(8,128)(2,1)}, u32[]{:S(2)}, u32[]{:S(2)}) %all-to-all-start.1) | async-done | bytes 4128800 | tf_op jit(solution)/shard_map/all_to_all | solution.py:39
  459.2 7.3 %reshape.72 = bf16[1152,1792]{1,0:T(8,128)(2,1)} reshape(bf16[64,18,1792]{2,1,0:T(8,128)(2,1)} %all-to-all-done.1) | data formatting | bytes 8257536 | tf_op jit(solution)/shard_map/reshape | solution.py:40
  466.5 10.6 %gather_fusion.1 = bf16[1024,1792]{1,0:T(8,128)(2,1)} fusion(bf16[1152,1792]{1,0:T(8,128)(2,1)} %reshape.72, s32[1024]{0:T(1024)S(1)} %broadcast_clamp_fusion), kind=kCustom, calls=%fused_computation.1 | custom fusion | bytes 7344128 | tf_op jit(solution)/shard_map/gather | solution.py:40
  477.2 6.1 %fusion = bf16[128,1792]{1,0:T(8,128)(2,1)} fusion(bf16[1024,1792]{1,0:T(8,128)(2,1)} %gather_fusion.1, f32[128,8]{1,0:T(8,128)S(1)} %copy.13), kind=kLoop, calls=%fused_computation.5 | loop fusion | flops 5275648 | bytes 4132864 | tf_op jit(solution)/shard_map/reduce_sum | solution.py:42
  (9 shorter events, 0.1 us)
Async XLA Ops:
  45.2 137.3 %all-to-all-start = ((bf16[64,18,1792]{2,1,0:T(8,128)(2,1)}), bf16[64,18,1792]{2,1,0:T(8,128)(2,1)}, u32[]{:S(2)}, u32[]{:S(2)}) async-start(bf16[64,18,1792]{2,1,0:T(8,128)(2,1)} %reshape.69), calls=%async_computation | async-start | bytes 11010048 | tf_op jit(solution)/shard_map/all_to_all | solution.py:29
  58.5 248.1 %all-reduce.3.cloned.1.call-start = ((), (), s32[]{:S(2)}) async-start(), calls=%async_computation.2 | async-start | bytes 9437184 | tf_op jit(solution)/shard_map/psum | solution.py:35
  306.6 3.7 copy-start.1
  324.2 11.0 %copy-start = (bf16[128,8]{0,1:T(8,128)(2,1)S(1)}, bf16[128,8]{0,1:T(8,128)(2,1)}, u32[]{:S(2)}) copy-start(bf16[128,8]{0,1:T(8,128)(2,1)} %param.10) | copy-start | bytes 6148
  324.2 135.0 %all-to-all-start.1 = ((bf16[64,18,1792]{2,1,0:T(8,128)(2,1)}), bf16[64,18,1792]{2,1,0:T(8,128)(2,1)}, u32[]{:S(2)}, u32[]{:S(2)}) async-start(bf16[64,18,1792]{2,1,0:T(8,128)(2,1)} %reshape.71), calls=%async_computation.1 | async-start | bytes 11010048 | tf_op jit(solution)/shard_map/all_to_all | solution.py:39
Sparse Core Ops, SparseCore 0:
  203.7 102.8 all-reduce.2

commit v2 on v1

v2 whole, which is shorter than its diff:
```python
import jax
import jax.numpy as jnp
from jax import lax
from jax.sharding import Mesh, PartitionSpec as P

N_Y, N_Z, N_C = 4, 8, 2
N_YC = N_Y * N_C
CHUNKS = 2
BF16 = jnp.bfloat16
F32 = jnp.float32


def routing_table(route_ids, route_weight, swap_flags):
    tok_rows = route_ids.shape[0]
    experts = swap_flags.shape[0]
    half = experts // 2
    hit = route_ids[:, :, None] == jnp.arange(experts, dtype=jnp.int32)
    named = jnp.any(hit, axis=1).astype(F32)
    weight = jnp.sum(jnp.where(hit, route_weight.astype(F32)[:, :, None], 0.0), axis=1)
    swapped = swap_flags[None, :] == 1
    named = jnp.where(swapped, jnp.roll(named, half, axis=1), named)
    weight = jnp.where(swapped, jnp.roll(weight, half, axis=1), weight)
    upto = jnp.tril(jnp.ones((tok_rows, tok_rows), BF16))
    place = jnp.dot(upto, named.astype(BF16), preferred_element_type=F32) * named
    return jnp.concatenate([place, weight], axis=1).astype(BF16)


def body(tokens, gate_up, down, route_ids, route_weight, swap_flags):
    tok_rows, feat_width = tokens.shape
    experts = swap_flags.shape[0]
    hidden_units = down.shape[1]
    top = route_ids.shape[1]
    capacity = min(tok_rows, 9 * tok_rows * top // (8 * experts))
    flat_gu = gate_up[0].reshape(feat_width, 2 * hidden_units)
    dn = down[0]
    my_z = lax.axis_index("z")

    table = routing_table(route_ids, route_weight, swap_flags)
    wide = jnp.concatenate([tokens, table], axis=1)
    column = lax.all_gather(wide, "z", axis=0, tiled=True)
    dest = jnp.arange(N_YC, dtype=jnp.int32)
    plane = ((dest // N_C) * N_Z + my_z) * N_C + dest % N_C
    pick = (jnp.arange(experts, dtype=jnp.int32)[:, None] == plane[None, :]).astype(BF16)
    places = jnp.dot(column[:, feat_width:feat_width + experts], pick, preferred_element_type=F32)
    weights = jnp.dot(column[:, feat_width + experts:], pick, preferred_element_type=F32)

    per = N_Z // CHUNKS
    rows = per * capacity
    toks = per * tok_rows
    sums = []
    row = jnp.arange(rows, dtype=jnp.int32)
    tok = jnp.arange(toks, dtype=jnp.int32)
    same = (row // capacity)[:, None] == (tok // tok_rows)[None, :]
    want = (row % capacity + 1).astype(F32)
    for chunk in range(CHUNKS):
        part = slice(chunk * toks, (chunk + 1) * toks)
        p, w = places[part].T, weights[part].T
        chosen = same[None] & (p[:, None, :] == want[None, :, None])
        gather = chosen.astype(BF16).reshape(N_YC * rows, toks)
        scatter = jnp.where(chosen, w[:, None, :], 0.0).astype(BF16).reshape(N_YC * rows, toks)
        outgoing = jnp.dot(gather, column[part, :feat_width], preferred_element_type=F32).astype(BF16)
        received = lax.all_to_all(outgoing.reshape(N_YC, rows, feat_width), ("y", "c"), 0, 0, tiled=True)
        received = received.reshape(N_YC * rows, feat_width)
        partial = jnp.dot(received, flat_gu, preferred_element_type=F32).astype(BF16)
        pre = lax.psum_scatter(partial, "x", scatter_dimension=0, tiled=True).astype(F32)
        hidden = (jax.nn.silu(pre[:, :hidden_units]) * pre[:, hidden_units:]).astype(BF16)
        hidden = lax.all_gather(hidden, "x", axis=0, tiled=True)
        result = jnp.dot(hidden, dn, preferred_element_type=F32).astype(BF16)
        back = lax.all_to_all(result.reshape(N_YC, rows, feat_width), ("y", "c"), 0, 0, tiled=True)
        back = back.reshape(N_YC * rows, feat_width)
        sums.append(lax.dot_general(scatter, back, (((0,), (0,)), ((), ())), preferred_element_type=F32).astype(BF16))
    return lax.psum_scatter(jnp.concatenate(sums, axis=0), "z", scatter_dimension=0, tiled=True)


def solution(mesh):
    grid = Mesh(mesh.devices.reshape(mesh.devices.shape[0], N_Y, N_Z, N_C), ("x", "y", "z", "c"))
    expert = ("y", "z", "c")
    return jax.shard_map(
        body,
        mesh=grid,
        in_specs=(
            P(expert, "x"),
            P(expert, "x", None, None),
            P(expert, None, "x"),
            P(expert, None),
            P(expert, None),
            P(),
        ),
        out_specs=P(expert, "x"),
        check_vma=False,
    )
```

time: 491 us -> 342 us (0.70)
  waiting for transfers between devices: 331 us -> 219 us
  local copies, waits for them, and re-layouts: 71.4 us -> 11.3 us
  blocking collectives: 0 us -> 29.5 us
  matrix products: 20.3 us -> 42.4 us
  other arithmetic: 28.9 us -> 9.66 us
  starting transfers between devices: 24.5 us -> 16.3 us
    all_to_all x2 -> x3, waiting for transfers between devices: 228 us -> 41.4 us  [the longest x2 24.5 us: body(): lax.all_to_all(result.reshape(N_YC, rows, feat_width), ('y', 'c'), 0, 0,...]
    psum x1 -> x0, waiting for transfers between devices: 103 us -> none  [body(): lax.psum(partial_value.astype(jnp.bfloat16), 'dp').astype(jnp.float32)]
    all_gather x0 -> x3, waiting for transfers between devices: none -> 98.7 us  [the longest x1 56.1 us: body(): column = lax.all_gather(wide, 'z', axis=0, tiled=True)]
    reduce_scatter x0 -> x3, waiting for transfers between devices: none -> 78.7 us  [the longest x1 49.5 us: body(): lax.psum_scatter(jnp.concatenate(sums, axis=0), 'z', scatter_dimension=0,...]
    all_to_all x0 -> x1, blocking collectives: none -> 29.5 us  [body(): lax.all_to_all(outgoing.reshape(N_YC, rows, feat_width), ('y', 'c'), 0, 0...]
    reshape x4 -> x0, local copies, waits for them, and re-layouts: 29.2 us -> none  [the longest x1 7.34 us: body(): row_block = received.reshape(senders * item_count, feat_width)]
    dot_general x2 -> x11, matrix products: 20.3 us -> 42.4 us  [the longest x2 14.4 us: body(): jnp.dot(received, flat_gu, preferred_element_type=F32).astype(BF16)]
    another operation x3 -> x1, other arithmetic: 18.2 us -> 0.08 us
  transfers between devices with their start and end apart: 3 -> 9, of which waited for: 3 -> 8; matrix products, arithmetic and copies ran while one was open for 4% -> 11% of each run, Pallas kernels for 0% -> 0%
where the time goes in v2:
time: 342 us
  waiting for transfers between devices  219 us (64%)
  matrix products  42.4 us (12%)
  blocking collectives  29.5 us (9%)
  starting transfers between devices  16.3 us (5%)
  between operations  13.6 us (4%)
  local copies, waits for them, and re-layouts  11.3 us (3%)
  other arithmetic  9.66 us (3%)
    all_gather x1, waiting for transfers between devices, body(): column = lax.all_gather(wide, 'z', axis=0, tiled=True)  56.1 us
    reduce_scatter x1, waiting for transfers between devices, body(): lax.psum_scatter(jnp.concatenate(sums, axis=0), 'z', scatter_dimension=0,...  49.5 us
    all_gather x2, waiting for transfers between devices, body(): hidden = lax.all_gather(hidden, 'x', axis=0, tiled=True)  42.6 us
    all_to_all x1, blocking collectives, body(): lax.all_to_all(outgoing.reshape(N_YC, rows, feat_width), ('y', 'c'), 0, 0...  29.5 us
    reduce_scatter x2, waiting for transfers between devices, body(): lax.psum_scatter(partial, 'x', scatter_dimension=0, tiled=True).astype(F32)  29.2 us
    all_to_all x2, waiting for transfers between devices, body(): lax.all_to_all(result.reshape(N_YC, rows, feat_width), ('y', 'c'), 0, 0,...  24.5 us
    all_to_all x1, waiting for transfers between devices, body(): lax.all_to_all(outgoing.reshape(N_YC, rows, feat_width), ('y', 'c'), 0, 0...  16.9 us
    dot_general x2, matrix products, body(): jnp.dot(received, flat_gu, preferred_element_type=F32).astype(BF16)  14.4 us
  transfers between devices with their start and end apart: 9, of which 8 were waited for; matrix products, arithmetic and copies ran while one was open for 11% of the time, Pallas kernels for 0%

profile of v2, /device:TPU:1, one launch (start us, length us, event | category | flops | bytes accessed | tf_op | source)
XLA Modules:
  0.0 341.7 jit_solution(14515367830078108722)
XLA Ops:
  6.5 0.7 broadcast_compare_fusion.1
  7.2 0.7 convert_element_type.70
  7.9 0.7 fusion.29
  8.6 0.7 select_reduce_fusion
  9.3 0.1 fusion.32
  9.4 0.1 copy.12
  9.6 0.2 fusion.12
  9.8 0.1 copy.11
  9.9 1.9 concatenate.18
  11.8 0.1 eq.136
  12.0 0.1 broadcast_compare_fusion
  12.1 56.1 %all-gather.4.cloned.1.call-done = bf16[1024,1920]{1,0:T(8,128)(2,1)} async-done(((bf16[128,1920]{1,0:T(8,128)(2,1)}), bf16[1024,1920]{1,0:T(8,128)(2,1)}) %all-gather.4.cloned.1.call-update) | async-done | bytes 3932176 | tf_op jit(solution)/shard_map/all_gather | solution.py:40
  68.1 1.1 fusion.27
  69.3 0.5 bitcast_and_fusion.1
  69.8 4.1 %convolution_convert_fusion.3 = bf16[576,1792]{1,0:T(8,128)(2,1)} fusion(pred[576,512]{1,0:T(32,128)(4,1)S(1)} %get-tuple-element.5, bf16[1024,1920]{1,0:T(8,128)(2,1)} %all-gather.4.cloned.1.call-done), kind=kOutput, calls=%fused_computation.12 | convolution fusion | flops 1057996800 | bytes 4194304 | tf_op jit(solution)/shard_map/dot_general | solution.py:61
  73.9 5.0 %all-to-all-start = ((bf16[8,72,1792]{2,1,0:T(8,128)(2,1)}), bf16[8,72,1792]{2,1,0:T(8,128)(2,1)S(1)}, u32[]{:S(2)}, u32[]{:S(2)}) async-start(bf16[8,72,1792]{2,1,0:T(8,128)(2,1)} %bitcast.59), calls=%async_computation | async-start | bytes 4128768 | tf_op jit(solution)/shard_map/all_to_all | solution.py:62
  78.9 9.1 %copy.13 = bf16[224,8,2,1024]{3,1,2,0:T(8,128)(2,1)} copy(bf16[224,8,2,1024]{3,2,1,0:T(2,128)(2,1)} %bitcast.51) | data formatting | bytes 14680064
  88.0 16.9 %all-to-all-done = bf16[8,72,1792]{2,1,0:T(8,128)(2,1)S(1)} async-done(((bf16[8,72,1792]{2,1,0:T(8,128)(2,1)}), bf16[8,72,1792]{2,1,0:T(8,128)(2,1)S(1)}, u32[]{:S(2)}, u32[]{:S(2)}) %all-to-all-start) | async-done | bytes 2064416 | tf_op jit(solution)/shard_map/all_to_all | solution.py:62
  104.9 8.8 %convolution_convert_fusion.2 = bf16[576,2048]{1,0:T(8,128)(2,1)} fusion(bf16[576,1792]{1,0:T(8,128)(2,1)S(1)} %bitcast.57, bf16[1792,2048]{1,0:T(8,128)(2,1)} %bitcast.52), kind=kOutput, calls=%fused_computation.11 | convolution fusion | flops 4229038080 | bytes 11763712 | tf_op jit(solution)/shard_map/dot_general | solution.py:64
  113.6 0.0 reduce-scatter.4.cloned.1.call-update
  113.6 0.0 reduce-scatter.6.cloned.1.call-start
  113.7 2.9 convolution_convert_fusion.1
  116.6 29.5 %all_to_all.20 = bf16[8,72,1792]{2,1,0:T(8,128)(2,1)S(1)} all-to-all(bf16[8,72,1792]{2,1,0:T(8,128)(2,1)S(1)} %bitcast.61), channel_id=1, replica_groups=mesh['x'=4,'y'=4,'z'=8,'c'=2] {'y','c'}, dimensions={0} | all-to-all | bytes 4128768 | tf_op jit(solution)/shard_map/all_to_all | solution.py:62
  146.1 5.7 %convolution_convert_fusion = bf16[576,2048]{1,0:T(8,128)(2,1)} fusion(bf16[576,1792]{1,0:T(8,128)(2,1)S(1)} %bitcast.60, bf16[1792,2048]{1,0:T(8,128)(2,1)S(1)} %bitcast.55), kind=kOutput, calls=%fused_computation.9 | convolution fusion | flops 4229038080 | bytes 11763712 | tf_op jit(solution)/shard_map/dot_general | solution.py:64
  151.7 0.0 reduce-scatter.6.cloned.1.call-update
  151.8 0.0 all-gather.6.cloned.1.call-start
  151.8 0.0 reduce-scatter.4.cloned.1.call-done
  151.8 1.2 convert_element_type.75
  153.0 0.9 fusion.14
  153.9 0.0 all-gather.6.cloned.1.call-update
  154.0 0.2 all-gather.8.cloned.1.call-start
  154.2 29.2 %reduce-scatter.6.cloned.1.call-done = bf16[144,2048]{1,0:T(8,128)(2,1)} async-done(((bf16[576,2048]{1,0:T(8,128)(2,1)}), bf16[144,2048]{1,0:T(8,128)(2,1)}) %reduce-scatter.6.cloned.1.call-update) | async-done | bytes 589840 | tf_op jit(solution)/shard_map/reduce_scatter | solution.py:65
  183.3 1.2 convert_element_type.82
  184.5 0.9 fusion.13
  185.4 0.0 all-gather.8.cloned.1.call-update
  185.4 25.3 %all-gather.6.cloned.1.call-done = bf16[576,1024]{1,0:T(8,128)(2,1)} async-done(((bf16[144,1024]{1,0:T(8,128)(2,1)}), bf16[576,1024]{1,0:T(8,128)(2,1)}) %all-gather.6.cloned.1.call-update) | async-done | bytes 1179664 | tf_op jit(solution)/shard_map/all_gather | solution.py:67
  210.7 6.0 %fusion.4 = bf16[576,1792]{1,0:T(8,128)(2,1)} fusion(bf16[576,1024]{1,0:T(8,128)(2,1)} %all-gather.6.cloned.1.call-done, bf16[1,1024,1792]{2,1,0:T(8,128)(2,1)} %param.8), kind=kOutput, calls=%fused_computation.7 | convolution fusion | flops 2114961408 | bytes 6914048 | tf_op jit(solution)/shard_map/dot_general | solution.py:68
  216.7 5.9 %all-to-all-start.1 = ((bf16[8,72,1792]{2,1,0:T(8,128)(2,1)}), bf16[8,72,1792]{2,1,0:T(8,128)(2,1)S(1)}, u32[]{:S(2)}, u32[]{:S(2)}) async-start(bf16[8,72,1792]{2,1,0:T(8,128)(2,1)} %bitcast.58), calls=%async_computation.2 | async-start | bytes 4128768 | tf_op jit(solution)/shard_map/all_to_all | solution.py:69
  222.6 17.3 %all-gather.8.cloned.1.call-done = bf16[576,1024]{1,0:T(8,128)(2,1)} async-done(((bf16[144,1024]{1,0:T(8,128)(2,1)}), bf16[576,1024]{1,0:T(8,128)(2,1)}) %all-gather.8.cloned.1.call-update) | async-done | bytes 1179664 | tf_op jit(solution)/shard_map/all_gather | solution.py:67
  239.9 6.0 %fusion.7 = bf16[576,1792]{1,0:T(8,128)(2,1)} fusion(bf16[576,1024]{1,0:T(8,128)(2,1)} %all-gather.8.cloned.1.call-done, bf16[1,1024,1792]{2,1,0:T(8,128)(2,1)} %param.8), kind=kOutput, calls=%fused_computation.8 | convolution fusion | flops 2114961408 | bytes 6914048 | tf_op jit(solution)/shard_map/dot_general | solution.py:68
  246.0 2.6 all-to-all-done.1
  248.6 5.1 %all-to-all-start.3 = ((bf16[8,72,1792]{2,1,0:T(8,128)(2,1)}), bf16[8,72,1792]{2,1,0:T(8,128)(2,1)}, u32[]{:S(2)}, u32[]{:S(2)}) async-start(bf16[8,72,1792]{2,1,0:T(8,128)(2,1)} %bitcast.56), calls=%async_computation.5 | async-start | bytes 4128768 | tf_op jit(solution)/shard_map/all_to_all | solution.py:69
  253.7 1.2 fusion.25
  255.0 3.0 bitcast_convert_fusion.1
  257.9 21.9 %all-to-all-done.3 = bf16[8,72,1792]{2,1,0:T(8,128)(2,1)} async-done(((bf16[8,72,1792]{2,1,0:T(8,128)(2,1)}), bf16[8,72,1792]{2,1,0:T(8,128)(2,1)}, u32[]{:S(2)}, u32[]{:S(2)}) %all-to-all-start.3) | async-done | bytes 2064416 | tf_op jit(solution)/shard_map/all_to_all | solution.py:69
  279.8 3.4 bitcast_convert_fusion
  283.3 2.0 pad_maximum_fusion
  285.3 49.5 %reduce-scatter.8.cloned.1.call-done = bf16[128,1792]{1,0:T(8,128)(2,1)} async-done(((bf16[1024,1792]{1,0:T(8,128)(2,1)}), bf16[128,1792]{1,0:T(8,128)(2,1)}) %reduce-scatter.8.cloned.1.call-update) | async-done | bytes 458768 | tf_op jit(solution)/shard_map/reduce_scatter | solution.py:72
  (22 shorter events, 0.1 us)
Async XLA Ops:
  6.5 61.6 %all-gather.4.cloned.1.call-start = ((), (), s32[]{:S(2)}) async-start(), calls=%async_computation.7 | async-start | bytes 4423680 | tf_op jit(solution)/shard_map/all_gather | solution.py:40
  73.9 30.9 %all-to-all-start = ((bf16[8,72,1792]{2,1,0:T(8,128)(2,1)}), bf16[8,72,1792]{2,1,0:T(8,128)(2,1)S(1)}, u32[]{:S(2)}, u32[]{:S(2)}) async-start(bf16[8,72,1792]{2,1,0:T(8,128)(2,1)} %bitcast.59), calls=%async_computation | async-start | bytes 4128768 | tf_op jit(solution)/shard_map/all_to_all | solution.py:62
  78.9 73.0 %reduce-scatter.4.cloned.1.call-start = ((), (), s32[]{:S(2)}) async-start(), calls=%async_computation.8 | async-start | bytes 2949120 | tf_op jit(solution)/shard_map/reduce_scatter | solution.py:65
  113.6 32.5 %slice-start = ((s8[7340032]{0:T(1024)(128)(4,1)}), s8[3145728]{0:T(1024)(128)(4,1)S(1)}, s32[]{:S(2)}) async-start(s8[7340032]{0:T(1024)(128)(4,1)} %bitcast.53), calls=%async_computation.13 | async-start | bytes 6291456
  113.6 69.7 %reduce-scatter.6.cloned.1.call-start = ((), (), s32[]{:S(2)}) async-start(), calls=%async_computation.10 | async-start | bytes 2949120 | tf_op jit(solution)/shard_map/reduce_scatter | solution.py:65
  113.7 32.4 %slice-start.1 = ((s8[7340032]{0:T(1024)(128)(4,1)}), s8[4194304]{0:T(1024)(128)(4,1)S(1)}, s32[]{:S(2)}) async-start(s8[7340032]{0:T(1024)(128)(4,1)} %bitcast.53), calls=%async_computation.14 | async-start | bytes 8388608
  151.8 59.0 %all-gather.6.cloned.1.call-start = ((), (), s32[]{:S(2)}) async-start(), calls=%async_computation.9 | async-start | bytes 1474560 | tf_op jit(solution)/shard_map/all_gather | solution.py:67
  154.0 86.0 %all-gather.8.cloned.1.call-start = ((), (), s32[]{:S(2)}) async-start(), calls=%async_computation.11 | async-start | bytes 1474560 | tf_op jit(solution)/shard_map/all_gather | solution.py:67
  216.7 31.9 %all-to-all-start.1 = ((bf16[8,72,1792]{2,1,0:T(8,128)(2,1)}), bf16[8,72,1792]{2,1,0:T(8,128)(2,1)S(1)}, u32[]{:S(2)}, u32[]{:S(2)}) async-start(bf16[8,72,1792]{2,1,0:T(8,128)(2,1)} %bitcast.58), calls=%async_computation.2 | async-start | bytes 4128768 | tf_op jit(solution)/shard_map/all_to_all | solution.py:69
  248.6 31.2 %all-to-all-start.3 = ((bf16[8,72,1792]{2,1,0:T(8,128)(2,1)}), bf16[8,72,1792]{2,1,0:T(8,128)(2,1)}, u32[]{:S(2)}, u32[]{:S(2)}) async-start(bf16[8,72,1792]{2,1,0:T(8,128)(2,1)} %bitcast.56), calls=%async_computation.5 | async-start | bytes 4128768 | tf_op jit(solution)/shard_map/all_to_all | solution.py:69
  253.7 81.1 %reduce-scatter.8.cloned.1.call-start = ((), (), s32[]{:S(2)}) async-start(), calls=%async_computation.12 | async-start | bytes 4128768 | tf_op jit(solution)/shard_map/reduce_scatter | solution.py:72
  279.8 3.4 %copy-start = (bf16[512,1792]{1,0:T(8,128)(2,1)S(1)}, bf16[512,1792]{1,0:T(8,128)(2,1)}, u32[]{:S(2)}) copy-start(bf16[512,1792]{1,0:T(8,128)(2,1)} %bitcast_convert_fusion.1) | copy-start | bytes 5505028
Sparse Core Ops, SparseCore 0:
  11.9 56.1 all-gather.3
  113.8 31.3 reduce-scatter.3
  151.9 31.4 reduce-scatter.5
  185.0 25.6 all-gather.5
  212.4 27.5 all-gather.7
  285.4 49.3 reduce-scatter.7
